TPU v7x, 256 devices: a whole 4x4x8 slice. The times are simulated.
256 devices in a mesh: clip: 64 (over z, y, core), space: 2 (over x_hi), tm: 2 (over x_lo).
Axes of the slice: x: 4 (x_hi: 2, x_lo: 2; x = x_hi * 2 + x_lo), y: 4, z: 8, core: 2. Of those that a mesh axis runs over, the one named last changes fastest.
Arguments:
- gen_latent: bfloat16 [64, 4, 8, 128, 16], P('clip', 'tm', 'space'), may hold values from -6 to 6
- frame_counts: int32 [64], replicated, may hold values from 1 to 4, as said below
- owner_map: int32 [64], replicated, may hold values from 0 to 63, as said below
- w_in: bfloat16 [3, 3, 16, 512], replicated, may hold values from -0.5 to 0.5
- w_query: bfloat16 [512, 512], replicated
- w_key: bfloat16 [512, 512], replicated, may hold values from -0.25 to 0.25
- w_value: bfloat16 [512, 512], replicated, may hold values from -0.25 to 0.25
- w_out: bfloat16 [512, 512], replicated, may hold values from -0.25 to 0.25
- w_space: bfloat16 [3, 3, 512, 512], replicated, may hold values from -0.09375 to 0.09375
- w_time: bfloat16 [3, 512, 512], replicated, may hold values from -0.15625 to 0.15625
- w_head: bfloat16 [512, 12], replicated, may hold values from -0.25 to 0.25
Outputs:
- pixels: float32 [64, 4, 3, 16, 256], P('clip', 'tm', None, 'space')
Inputs may be any that keep to these rules, and one draw needn't show every extreme that they name: `frame_counts`: some clip has all 4 frames live. `owner_map`: each decoder slot is named once; some generator clip g goes to decoder slot (g + 32) mod 64.
All inputs are finite; a program needn't handle non-finite values.
Results may differ from a plain program's by a relative error of at most 0.027.
Values may be sent and summed in bfloat16 or wider, within the bound.
A program may use at most 64 MiB of HBM per device.

v0:
```python
import math

import jax
import jax.numpy as jnp
from jax import lax
from jax.sharding import PartitionSpec as P

EPS = 1e-06


def with_halo(block, sides, width):
    for axis, dim in sides:
        count = lax.axis_size(axis)
        forward = [(i, i + 1) for i in range(count - 1)]
        backward = [(target, source) for source, target in forward]
        low = lax.ppermute(
            lax.slice_in_dim(block, block.shape[dim] - width, None, axis=dim), axis, forward
        )
        high = lax.ppermute(lax.slice_in_dim(block, 0, width, axis=dim), axis, backward)
        block = jnp.concatenate([low, block, high], axis=dim)
    return block


def shifted(block, axis, distance):
    devices = range(lax.axis_size(axis))
    route = [(i - distance, i) for i in devices if i - distance in devices]
    return lax.ppermute(block, axis, route)


def normed(field):
    wide = field.astype(jnp.float32)
    return wide * lax.rsqrt(jnp.mean(wide * wide, axis=-1, keepdims=True) + EPS)


def spatial_conv(padded, weight):
    height = padded.shape[-3] - 2
    width = padded.shape[-2]
    side_pad = jnp.pad(padded, [(0, 0)] * (padded.ndim - 2) + [(1, 1), (0, 0)])
    result = None
    for row_step in range(3):
        for col_step in range(3):
            window = side_pad[..., row_step : row_step + height, col_step : col_step + width, :]
            term = jnp.dot(window, weight[row_step, col_step], preferred_element_type=jnp.float32)
            result = term if result is None else result + term
    return result


def inverse_haar(coeffs):
    lead = coeffs.shape[:-3]
    height, width = (coeffs.shape[-3], coeffs.shape[-2])
    low_low = coeffs[..., 0:3]
    low_high = coeffs[..., 3:6]
    high_low = coeffs[..., 6:9]
    high_high = coeffs[..., 9:12]
    even_even = (low_low + low_high + high_low + high_high) * 0.5
    even_odd = (low_low - low_high + high_low - high_high) * 0.5
    odd_even = (low_low + low_high - high_low - high_high) * 0.5
    odd_odd = (low_low - low_high - high_low + high_high) * 0.5
    upper = jnp.stack([even_even, even_odd], axis=-2).reshape(lead + (height, 2 * width, 3))
    lower = jnp.stack([odd_even, odd_odd], axis=-2).reshape(lead + (height, 2 * width, 3))
    joined = jnp.stack([upper, lower], axis=-3).reshape(lead + (2 * height, 2 * width, 3))
    return jnp.moveaxis(joined, -1, -3)


def body(
    gen_latent,
    frame_counts,
    owner_map,
    w_in,
    w_query,
    w_key,
    w_value,
    w_out,
    w_space,
    w_time,
    w_head,
):
    clip_index = lax.axis_index("clip")
    per_device = gen_latent.shape[0]
    slots = clip_index * per_device + jnp.arange(per_device, dtype=jnp.int32)
    select = (owner_map[None, :] == slots[:, None]).astype(jnp.bfloat16)
    latent = jnp.einsum(
        "jr,rthwc->jthwc",
        select,
        lax.all_gather(gen_latent, "clip", axis=0, tiled=True),
        preferred_element_type=jnp.float32,
    ).astype(jnp.bfloat16)
    matches = owner_map[None, :] == slots[:, None]
    live = jnp.sum(jnp.where(matches, frame_counts[None, :], 0), axis=1)
    padded = with_halo(latent, (("space", 2),), 1)
    first = spatial_conv(padded, w_in).astype(jnp.bfloat16)
    normal_in = normed(first).astype(jnp.bfloat16)
    queries = jnp.dot(normal_in, w_query, preferred_element_type=jnp.float32).astype(jnp.bfloat16)
    frame_index = lax.axis_index("tm")
    local_frames = gen_latent.shape[1]
    query_frames = frame_index * local_frames + jnp.arange(local_frames, dtype=jnp.int32)
    scale = 1.0 / math.sqrt(queries.shape[-1])
    keys = jnp.dot(normal_in, w_key, preferred_element_type=jnp.float32).astype(jnp.bfloat16)
    values = jnp.dot(normal_in, w_value, preferred_element_type=jnp.float32).astype(jnp.bfloat16)
    key_part = lax.all_gather(keys, "tm", axis=1, tiled=True)
    highest = jnp.full(first.shape[:-1], -1e30, jnp.float32)
    key_frames = jnp.arange(key_part.shape[1], dtype=jnp.int32)
    allowed = (query_frames[:, None] >= key_frames[None, :]) & (key_frames[None, :] >= 0)
    allowed = allowed[None, :, None, None, :]
    scores = (
        jnp.einsum("cthwd,cshwd->cthws", queries, key_part, preferred_element_type=jnp.float32)
        * scale
    )
    masked = jnp.where(allowed, scores, jnp.float32(-1e30))
    new_high = jnp.maximum(highest, jnp.max(masked, axis=-1))
    weights = jnp.where(allowed, jnp.exp(masked - new_high[..., None]), jnp.float32(0.0))
    total = jnp.sum(weights, axis=-1)
    summed = jnp.einsum(
        "cthws,cshwd->cthwd",
        weights.astype(jnp.bfloat16),
        lax.all_gather(values, "tm", axis=1, tiled=True),
        preferred_element_type=jnp.float32,
    )
    attended = (summed / total[..., None]).astype(jnp.bfloat16)
    second = (
        first.astype(jnp.float32) + jnp.dot(attended, w_out, preferred_element_type=jnp.float32)
    ).astype(jnp.bfloat16)
    activated = jax.nn.silu(normed(second)).astype(jnp.bfloat16)
    rimmed = with_halo(activated, (("space", 2),), 1)
    spread = spatial_conv(rimmed, w_space).astype(jnp.bfloat16)
    earlier = shifted(spread, "tm", 1)
    extended = jnp.concatenate([earlier, spread], axis=1)
    temporal = None
    for offset in range(3):
        term = jnp.dot(
            extended[:, offset : offset + local_frames],
            w_time[offset],
            preferred_element_type=jnp.float32,
        )
        temporal = term if temporal is None else temporal + term
    third = (second.astype(jnp.float32) + temporal).astype(jnp.bfloat16)
    coeffs = jnp.dot(third, w_head, preferred_element_type=jnp.float32)
    image = inverse_haar(coeffs)
    keep = (query_frames[None, :] < live[:, None]).astype(jnp.float32)
    return image * keep[:, :, None, None, None]


def solution(mesh):
    return jax.shard_map(
        body,
        mesh=mesh,
        in_specs=(
            P("clip", "tm", "space", None, None),
            P(),
            P(),
            P(),
            P(),
            P(),
            P(),
            P(),
            P(),
            P(),
            P(),
        ),
        out_specs=P("clip", "tm", None, "space", None),
        check_vma=False,
    )
```

profile of v0, /device:TPU:2, one launch (start us, length us, event | category | flops | bytes accessed | tf_op | source)
XLA Modules:
  0.0 256.6 jit_solution(17977231139100309869)
XLA Ops:
  7.3 83.1 %all-gather.6.cloned.1.call-done = bf16[64,2,4,128,16]{3,4,2,1,0:T(8,128)(2,1)} async-done(((bf16[1,2,4,128,16]{3,4,2,1,0:T(8,128)(2,1)}), bf16[64,2,4,128,16]{3,4,2,1,0:T(8,128)(2,1)}) %all-gather.6.cloned.1.call-update) | async-done | bytes 2097168 | tf_op jit(solution)/shard_map/all_gather | solution.py:85
  90.4 2.8 %fusion.12 = f32[1,2,4,128,16]{3,0,4,2,1:T(1,128)S(1)} fusion(bf16[64,2,4,128,16]{3,4,2,1,0:T(8,128)(2,1)} %all-gather.6.cloned.1.call-done, s32[64]{0:T(128)} %param.13, s32[]{:T(128)S(6)} %axis_index.23), kind=kOutput, calls=%fused_computation.21 | convolution fusion | flops 2097216 | bytes 2162948 | tf_op jit(solution)/shard_map/jr,rthwc->jthwc/dot_general | solution.py:82
  93.3 4.0 %collective-permute-start = (bf16[1,2,1,128,16]{3,4,2,1,0:T(8,128)(2,1)S(1)}, bf16[1,2,1,128,16]{3,4,2,1,0:T(8,128)(2,1)S(1)}, u32[]{:S(2)}, u32[]{:S(2)}) collective-permute-start(bf16[1,2,1,128,16]{3,4,2,1,0:T(8,128)(2,1)S(1)} %get-tuple-element.11), channel_id=1, source_target_pairs={{0,2},{1,3},{4,6},{5,7},{8,10},{9,11},{12,14},{13,15},{16,18},{17,... | collective-permute-start | bytes 24584 | tf_op jit(solution)/shard_map/ppermute | solution.py:16
  97.3 1.3 collective-permute-start.1
  99.0 5.3 %collective-permute-done.1 = bf16[1,2,1,128,16]{3,4,2,1,0:T(8,128)(2,1)S(1)} collective-permute-done((bf16[1,2,1,128,16]{3,4,2,1,0:T(8,128)(2,1)S(1)}, bf16[1,2,1,128,16]{3,4,2,1,0:T(8,128)(2,1)S(1)}, u32[]{:S(2)}, u32[]{:S(2)}) %collective-permute-start.1) | collective-permute-done | bytes 8224 | tf_op jit(solution)/shard_map/ppermute | solution.py:19
  109.0 1.8 convolution_convert_fusion.1
  111.1 1.8 convolution_convert_fusion.2
  113.0 1.8 convolution_convert_fusion
  114.7 29.5 %all-gather.10.cloned.1.call-done = bf16[4,4,128,512]{3,2,1,0:T(8,128)(2,1)} async-done(((bf16[2,4,128,512]{3,2,1,0:T(8,128)(2,1)}), bf16[4,4,128,512]{3,2,1,0:T(8,128)(2,1)}) %all-gather.10.cloned.1.call-update) | async-done | bytes 2097168 | tf_op jit(solution)/shard_map/all_gather | solution.py:100
  144.2 4.8 %fusion.152 = (f32[2,4,128]{0,2,1:T(8,128)S(1)}, f32[1,2,4,128,4]{4,1,3,2,0:T(2,128)S(1)}) fusion(bf16[2,4,128,512]{3,2,1,0:T(8,128)(2,1)} %convolution_convert_fusion, bf16[4,4,128,512]{3,2,1,0:T(8,128)(2,1)} %all-gather.10.cloned.1.call-done, pred[2,4]{1,0:T(4,128)(4,1)S(1)} %iota_compare_fusion.4), kind=kOutput, calls=%fused_computation.183 | convolution fusion | flops 4205568 | bytes 3166216 | tf_op jit(solution)/shard_map/cthwd,cshwd->cthws/dot_general | solution.py:106
  149.0 1.3 fusion.116
  150.3 34.9 %all-gather.8.cloned.1.call-done = bf16[4,4,128,512]{3,2,1,0:T(8,128)(2,1)} async-done(((bf16[2,4,128,512]{3,2,1,0:T(8,128)(2,1)}), bf16[4,4,128,512]{3,2,1,0:T(8,128)(2,1)}) %all-gather.8.cloned.1.call-update) | async-done | bytes 2097168 | tf_op jit(solution)/shard_map/all_gather | solution.py:116
  185.2 4.3 %fusion.53 = bf16[2,4,128,512]{3,0,2,1:T(2,128)(2,1)S(1)} fusion(f32[2,4,128]{0,2,1:T(8,128)S(1)} %fusion.116, bf16[4,4,128,512]{3,2,1,0:T(8,128)(2,1)} %all-gather.8.cloned.1.call-done, f32[1,2,4,128,4]{4,1,3,2,0:T(2,128)S(1)} %get-tuple-element.16, pred[2,4]{1,0:T(4,128)(4,1)S(1)} %iota_compare_fusion.4, f32[2,4,128]{0,2,1:T(8,128)S(1)} %broadcast_maximum_fusion), kind=kOutput, calls=%fused_computation.69 | convolution fusion | flops 5255168 | bytes 3170312 | tf_op jit(solution)/shard_map/cthws,cshwd->cthwd/dot_general | solution.py:113
  191.1 4.8 %collective-permute-start.2 = (bf16[1,2,1,128,512]{4,3,2,1,0:T(8,128)(2,1)S(1)}, bf16[1,2,1,128,512]{4,3,2,1,0:T(8,128)(2,1)S(1)}, u32[]{:S(2)}, u32[]{:S(2)}) collective-permute-start(bf16[1,2,1,128,512]{4,3,2,1,0:T(8,128)(2,1)S(1)} %get-tuple-element.5), channel_id=1, source_target_pairs={{0,2},{1,3},{4,6},{5,7},{8,10},{9,11},{12,14},{13,15},{16,18},{17,... | collective-permute-start | bytes 786440 | tf_op jit(solution)/shard_map/ppermute | solution.py:16
  195.9 1.6 collective-permute-start.3
  197.6 2.0 fusion.74
  199.6 1.9 collective-permute-done.2
  201.4 5.8 %collective-permute-done.3 = bf16[1,2,1,128,512]{4,3,2,1,0:T(8,128)(2,1)S(1)} collective-permute-done((bf16[1,2,1,128,512]{4,3,2,1,0:T(8,128)(2,1)S(1)}, bf16[1,2,1,128,512]{4,3,2,1,0:T(8,128)(2,1)S(1)}, u32[]{:S(2)}, u32[]{:S(2)}) %collective-permute-start.3) | collective-permute-done | bytes 262176 | tf_op jit(solution)/shard_map/ppermute | solution.py:19
  212.7 1.2 add_convert_fusion
  213.9 1.3 collective-permute-start.4
  217.2 22.3 %collective-permute-done.4 = bf16[1,2,4,128,512]{4,3,2,1,0:T(8,128)(2,1)S(1)} collective-permute-done((bf16[1,2,4,128,512]{4,3,2,1,0:T(8,128)(2,1)S(1)}, bf16[1,2,4,128,512]{4,3,2,1,0:T(8,128)(2,1)S(1)}, u32[]{:S(2)}, u32[]{:S(2)}) %collective-permute-start.4) | collective-permute-done | bytes 1048608 | tf_op jit(solution)/shard_map/ppermute | solution.py:27
  240.5 2.0 fusion.33
  242.5 3.3 %fusion.31 = f32[1,2,4,128,12]{3,4,2,1,0:T(8,128)S(1)} fusion(bf16[2,4,128,512]{3,2,1,0:T(8,128)(2,1)} %copy-done.2, f32[2,4,128,512]{3,2,1,0:T(8,128)S(1)} %fusion.65, f32[2,4,128,512]{3,2,1,0:T(8,128)} %fusion.33, bf16[1,2,4,128,512]{4,3,2,1,0:T(8,128)(2,1)} %copy-done.3, bf16[3,512,512]{2,1,0:T(8,128)(2,1)} %param.20, bf16[512,12]{0,1:T(8,128)(2,1)S(1)} %copy-done.6), kind=kOutput, calls=%fused_computation.42 | convolution fusion | flops 552075264 | bytes 6877184 | tf_op jit(solution)/shard_map/dot_general | solution.py:137
  247.6 1.3 pad_maximum_fusion
  (74 shorter events, 19.1 us)
Async XLA Ops:
  6.5 183.0 %copy-start = (bf16[512,512]{1,0:T(8,128)(2,1)S(1)}, bf16[512,512]{1,0:T(8,128)(2,1)}, u32[]{:S(2)}) copy-start(bf16[512,512]{1,0:T(8,128)(2,1)} %param.18) | copy-start | bytes 1572868
  6.5 92.0 %copy-start.5 = (bf16[3,3,16,512]{3,2,1,0:T(8,128)(2,1)S(1)}, bf16[3,3,16,512]{3,2,1,0:T(8,128)(2,1)}, u32[]{:S(2)}) copy-start(bf16[3,3,16,512]{3,2,1,0:T(8,128)(2,1)} %param.14) | copy-start | bytes 442372
  6.5 83.9 %all-gather.6.cloned.1.call-start = ((), (), s32[]{:S(2)}) async-start(), calls=%async_computation | async-start | bytes 2129920 | tf_op jit(solution)/shard_map/all_gather | solution.py:85
  7.3 136.9 %all-gather.10.cloned.1.call-start = ((), (), s32[]{:S(2)}) async-start(), calls=%async_computation.2 | async-start | bytes 3145728 | tf_op jit(solution)/shard_map/all_gather | solution.py:100
  93.3 5.8 %collective-permute-start = (bf16[1,2,1,128,16]{3,4,2,1,0:T(8,128)(2,1)S(1)}, bf16[1,2,1,128,16]{3,4,2,1,0:T(8,128)(2,1)S(1)}, u32[]{:S(2)}, u32[]{:S(2)}) collective-permute-start(bf16[1,2,1,128,16]{3,4,2,1,0:T(8,128)(2,1)S(1)} %get-tuple-element.11), channel_id=1, source_target_pairs={{0,2},{1,3},{4,6},{5,7},{8,10},{9,11},{12,14},{13,15},{16,18},{17,... | collective-permute-start | bytes 24584 | tf_op jit(solution)/shard_map/ppermute | solution.py:16
  97.3 7.0 %collective-permute-start.1 = (bf16[1,2,1,128,16]{3,4,2,1,0:T(8,128)(2,1)S(1)}, bf16[1,2,1,128,16]{3,4,2,1,0:T(8,128)(2,1)S(1)}, u32[]{:S(2)}, u32[]{:S(2)}) collective-permute-start(bf16[1,2,1,128,16]{3,4,2,1,0:T(8,128)(2,1)S(1)} %get-tuple-element.12), channel_id=1, source_target_pairs={{2,0},{3,1},{6,4},{7,5},{10,8},{11,9},{14,12},{15,13},{18,16},{19,... | collective-permute-start | bytes 24584 | tf_op jit(solution)/shard_map/ppermute | solution.py:19
  107.9 1.1 copy-start.9
  109.0 2.1 copy-start.10
  110.8 2.1 copy-start.11
  110.9 74.4 %all-gather.8.cloned.1.call-start = ((), (), s32[]{:S(2)}) async-start(), calls=%async_computation.1 | async-start | bytes 3145728 | tf_op jit(solution)/shard_map/all_gather | solution.py:116
  190.3 9.2 %copy-start.2 = (bf16[2,4,128,512]{3,2,1,0:T(8,128)(2,1)}, bf16[2,4,128,512]{3,2,1,0:T(8,128)(2,1)S(1)}, u32[]{:S(2)}) copy-start(bf16[2,4,128,512]{3,2,1,0:T(8,128)(2,1)S(1)} %get-tuple-element.18) | copy-start | bytes 3145732
  190.4 17.3 %slice-start = ((s8[4718592]{0:T(1024)(128)(4,1)}), s8[4194304]{0:T(1024)(128)(4,1)S(1)}, s32[]{:S(2)}) async-start(s8[4718592]{0:T(1024)(128)(4,1)} %bitcast.287), calls=%async_computation.3 | async-start | bytes 8388608
  191.1 10.3 %collective-permute-start.2 = (bf16[1,2,1,128,512]{4,3,2,1,0:T(8,128)(2,1)S(1)}, bf16[1,2,1,128,512]{4,3,2,1,0:T(8,128)(2,1)S(1)}, u32[]{:S(2)}, u32[]{:S(2)}) collective-permute-start(bf16[1,2,1,128,512]{4,3,2,1,0:T(8,128)(2,1)S(1)} %get-tuple-element.5), channel_id=1, source_target_pairs={{0,2},{1,3},{4,6},{5,7},{8,10},{9,11},{12,14},{13,15},{16,18},{17,... | collective-permute-start | bytes 786440 | tf_op jit(solution)/shard_map/ppermute | solution.py:16
  195.9 11.8 %slice-start.1 = ((s8[4718592]{0:T(1024)(128)(4,1)}), s8[524288]{0:T(1024)(128)(4,1)S(1)}, s32[]{:S(2)}) async-start(s8[4718592]{0:T(1024)(128)(4,1)} %bitcast.287), calls=%async_computation.4 | async-start | bytes 1048576
  195.9 11.3 %collective-permute-start.3 = (bf16[1,2,1,128,512]{4,3,2,1,0:T(8,128)(2,1)S(1)}, bf16[1,2,1,128,512]{4,3,2,1,0:T(8,128)(2,1)S(1)}, u32[]{:S(2)}, u32[]{:S(2)}) collective-permute-start(bf16[1,2,1,128,512]{4,3,2,1,0:T(8,128)(2,1)S(1)} %get-tuple-element.6), channel_id=1, source_target_pairs={{2,0},{3,1},{6,4},{7,5},{10,8},{11,9},{14,12},{15,13},{18,16},{19,... | collective-permute-start | bytes 786440 | tf_op jit(solution)/shard_map/ppermute | solution.py:19
  212.6 2.6 copy-start.7
  212.7 2.6 copy-start.8
  212.7 3.8 %copy-start.4 = (bf16[3,512,512]{2,1,0:T(8,128)(2,1)S(1)}, bf16[3,512,512]{2,1,0:T(8,128)(2,1)}, u32[]{:S(2)}) copy-start(bf16[3,512,512]{2,1,0:T(8,128)(2,1)} %param.20) | copy-start | bytes 4718596
  213.9 25.6 %collective-permute-start.4 = (bf16[1,2,4,128,512]{4,3,2,1,0:T(8,128)(2,1)S(1)}, bf16[1,2,4,128,512]{4,3,2,1,0:T(8,128)(2,1)S(1)}, u32[]{:S(2)}, u32[]{:S(2)}) collective-permute-start(bf16[1,2,4,128,512]{4,3,2,1,0:T(8,128)(2,1)S(1)} %bitcast.283), channel_id=1, source_target_pairs={{0,1},{2,3},{4,5},{6,7},{8,9},{10,11},{12,13},{14,15},{16,17},{18,... | collective-permute-start | bytes 3145736 | tf_op jit(solution)/shard_map/ppermute | solution.py:27
  217.2 25.3 %copy-start.6 = (bf16[512,12]{0,1:T(8,128)(2,1)S(1)}, bf16[512,12]{0,1:T(8,128)(2,1)}, u32[]{:S(2)}) copy-start(bf16[512,12]{0,1:T(8,128)(2,1)} %param.21) | copy-start | bytes 36868
  239.5 1.0 copy-start.3
  247.6 2.5 copy-start.1
Sparse Core Ops, SparseCore 0:
  10.1 80.2 all-gather.5
  111.0 33.1 all-gather.9
  146.0 39.1 all-gather.7
where the time goes:
time: 257 us
  waiting for transfers between devices  183 us (71%)
  matrix products  37.3 us (15%)
  between operations  13.5 us (5%)
  starting transfers between devices  13.3 us (5%)
  other arithmetic  5.36 us (2%)
  local copies, waits for them, and re-layouts  3.83 us (1%)
    all_gather x1, waiting for transfers between devices, body(): lax.all_gather(gen_latent, 'clip', axis=0, tiled=True)  83.1 us
    all_gather x1, waiting for transfers between devices, body(): lax.all_gather(values, 'tm', axis=1, tiled=True)  34.9 us
    all_gather x1, waiting for transfers between devices, body(): key_part = lax.all_gather(keys, 'tm', axis=1, tiled=True)  29.5 us
    ppermute x1, waiting for transfers between devices, shifted(): return lax.ppermute(block, axis, route)  22.3 us
    dot_general x18, matrix products, spatial_conv(): jnp.dot(window, weight[row_step, col_step], preferred_element_type=jnp.fl...  13.2 us
    ppermute x2, waiting for transfers between devices, with_halo(): lax.ppermute(lax.slice_in_dim(block, 0, width, axis=dim), axis, backward)  11.1 us
    ppermute x2, starting transfers between devices, with_halo(): lax.ppermute(lax.slice_in_dim(block, block.shape[dim] - width, None, axis...  8.78 us
  transfers between devices with their start and end apart: 8, of which 7 were waited for; matrix products, arithmetic and copies ran while one was open for 6% of the time, Pallas kernels for 0%

commit v1 on v0

v1 whole, which is shorter than its diff:
```python
import functools
import math

import jax
import jax.numpy as jnp
from jax import lax
from jax.experimental import pallas as pl
from jax.experimental.pallas import tpu as pltpu
from jax.sharding import PartitionSpec as P

EPS = 1e-06
MESH = pl.DeviceIdType.MESH
F32 = jnp.float32
BF16 = jnp.bfloat16
WIDE = 128
PAIR = 2 * WIDE


def dot(a, b):
    return jnp.dot(a, b, preferred_element_type=F32)


def dot_nt(a, b):
    return lax.dot_general(a, b, (((1,), (1,)), ((), ())), preferred_element_type=F32)


def kernel(
    plane,
    planes,
    owner,
    counts,
    lat,
    w_in,
    w_query,
    w_key,
    w_value,
    w_out,
    w_space,
    w_time,
    w_head,
    out,
    v_in,
    v_query,
    v_key,
    v_value,
    v_out,
    v_space,
    v_time,
    v_head,
    in_t,
    head16,
    qk_t,
    vo_t,
    taps,
    eff,
    spread_cols,
    gat_a,
    gat_b,
    p_buf,
    got_a,
    got_b,
    quarter,
    panel,
    patches,
    first,
    normal,
    query,
    mixed,
    active,
    head_sum,
    parts,
    total,
    total16,
    from_tm,
    from_edge,
    owned,
    pixel_rows,
    w_sem,
    own_sem,
    g_send,
    g_recv,
    p_send,
    p_recv,
    x_send,
    x_recv,
    o_send,
    o_recv,
):
    ch = v_query.shape[0]
    me = lax.axis_index("clip")
    s = lax.axis_index("space")
    t = lax.axis_index("tm")
    m = lax.rem(me, plane)
    z = me // plane
    base = z * plane
    gat = (gat_a, gat_b)
    got = (got_a, got_b)

    loads = [
        pltpu.make_async_copy(src, dst, w_sem.at[i])
        for i, (src, dst) in enumerate(
            (
                (w_key, v_key),
                (w_query, v_query),
                (w_value, v_value),
                (w_out, v_out),
                (w_head, v_head),
                (w_in, v_in),
                (w_time, v_time),
                (w_space, v_space),
            )
        )
    ]
    l_key, l_query, l_value, l_out, l_head, l_in, l_time, l_space = loads

    def plane_peer(d):
        return (base + lax.rem(m + d, plane), s, t)

    def column_peer(d):
        return (lax.rem(z + d, planes) * plane + m, s, t)

    x_peers = [(me, s, 1 - t), (me, 1 - s, t), (me, 1 - s, 1 - t)]
    everyone = [plane_peer(d) for d in range(1, plane)]
    everyone += [column_peer(d) for d in range(1, planes)] + x_peers
    barrier = pltpu.get_barrier_semaphore()
    for peer in everyone:
        pl.semaphore_signal(barrier, inc=1, device_id=peer, device_id_type=MESH)
    ways = ((planes, column_peer, z), (plane, plane_peer, m))
    own = [
        pltpu.make_async_copy(lat.at[c], gat[c].at[ways[c][2]], own_sem.at[c]) for c in range(2)
    ]
    for copy in own + loads:
        copy.start()
    pl.semaphore_wait(barrier, len(everyone))

    gathers = ([], [])
    for c in range(2):
        count, peer, place = ways[c]
        for d in sorted(range(1, count), key=lambda d: -min(d, count - d)):
            copy = pltpu.make_async_remote_copy(
                src_ref=lat.at[c],
                dst_ref=gat[c].at[place],
                send_sem=g_send.at[c, d],
                recv_sem=g_recv.at[c, d],
                device_id=peer(d),
                device_id_type=MESH,
            )
            copy.start()
            gathers[c].append(copy)

    picks = ([], [])
    for d in range(plane):
        slot = base + lax.rem(m + d, plane)
        pick = jnp.int32(0)
        for i in range(planes):
            pick = jnp.where(owner[i * plane + m] == slot, jnp.int32(i), pick)
        picks[0].append(pick)
    for d in range(planes):
        slot = lax.rem(z + d, planes) * plane + m
        pick = jnp.int32(0)
        for i in range(plane):
            pick = jnp.where(owner[base + i] == slot, jnp.int32(i), pick)
        picks[1].append(pick)

    def scan(g, carry):
        from_a, from_b, live = carry
        here = owner[g] == me
        step_a = lax.rem(m - lax.rem(g, plane) + plane, plane)
        step_b = lax.rem(z - g // plane + planes, planes)
        return (
            jnp.where(here, step_a, from_a),
            jnp.where(here, step_b, from_b),
            jnp.where(here, counts[g], live),
        )

    from_a, from_b, live = lax.fori_loop(0, plane * planes, scan, (jnp.int32(0),) * 3)

    l_key.wait()
    l_query.wait()
    qk_t[...] = dot_nt(v_key[...], v_query[...]).astype(BF16)
    l_value.wait()
    l_out.wait()
    vo_t[0:ch, :] = dot(v_value[...], v_out[...]).T.astype(BF16)

    passes = []
    for c in (1, 0):
        count, peer, _ = ways[1 - c]
        own[c].wait()
        for copy in gathers[c]:
            copy.wait_recv()
        for d in sorted(range(count), key=lambda d: -min(d, count - d)):
            block = gat[c][picks[c][d]]
            if d == 0:
                got[c][0] = block
                continue
            p_buf[c, d] = block
            copy = pltpu.make_async_remote_copy(
                src_ref=p_buf.at[c, d],
                dst_ref=got[c].at[d],
                send_sem=p_send.at[c, d],
                recv_sem=p_recv.at[c, d],
                device_id=peer(d),
                device_id_type=MESH,
            )
            copy.start()
            passes.append(copy)

    l_head.wait()
    wide = v_head[...].astype(F32)
    gap = jnp.zeros((1, ch), F32)
    head16[...] = jnp.concatenate(
        [wide[0:3], gap, wide[3:6], gap, wide[6:9], gap, wide[9:12], gap], axis=0
    ).astype(BF16)
    l_in.wait()
    in_t[0:ch, :] = v_in[...].astype(F32).T.astype(BF16)
    in_t[ch : ch + 16, :] = dot_nt(head16[...], v_in[...]).astype(BF16)
    vo_t[ch : ch + 16, :] = dot(head16[...], vo_t[0:ch, :]).astype(BF16)
    l_time.wait()
    for k in range(3):
        taps[16 * k : 16 * k + 16, :] = dot_nt(head16[...], v_time[k]).astype(BF16)
    l_space.wait()

    def fold(i, carry):
        eff[i] = dot_nt(taps[...], v_space[i]).astype(BF16)
        return carry

    lax.fori_loop(0, 6, fold, 0)

    for copy in passes:
        copy.wait_recv()
    quarter[0] = got_a[from_a]
    quarter[1] = got_b[from_b]

    def exchange(i, src, dst, peer, sems):
        copy = pltpu.make_async_remote_copy(
            src_ref=src,
            dst_ref=dst,
            send_sem=sems[0].at[i],
            recv_sem=sems[1].at[i],
            device_id=peer,
            device_id_type=MESH,
        )
        copy.start()
        return copy

    frames = pl.ds(2 * t, 2)
    sems = (x_send, x_recv)
    rows = [
        exchange(0, quarter.at[:, pl.ds(1 - t, 3)], panel.at[frames, pl.ds(t, 3)], x_peers[0], sems),
        exchange(1, quarter.at[:, 3 * (1 - s)], panel.at[frames, 3 * t], x_peers[1], sems),
        exchange(2, quarter.at[:, 3 * (1 - s)], panel.at[frames, 3 * (1 - t)], x_peers[2], sems),
    ]
    for f in range(2):
        for r in range(3):
            panel[2 * t + f, 1 - t + r] = quarter[f, t + r]

    lax.fori_loop(6, 9, fold, 0)
    r_id = lax.broadcasted_iota(jnp.int32, (PAIR, PAIR), 0)
    c_id = lax.broadcasted_iota(jnp.int32, (PAIR, PAIR), 1)
    goal = jnp.where(r_id < WIDE, 2 * r_id, 2 * (r_id - WIDE) + 1)
    spread_cols[...] = jnp.where(goal == c_id, 1.0, 0.0).astype(BF16)
    parts[...] = jnp.zeros(parts.shape, F32)

    for copy in rows:
        copy.wait_recv()

    lane = lax.broadcasted_iota(jnp.int32, (16, WIDE), 1)
    top = jnp.logical_not(jnp.logical_and(s == 0, t == 0))
    bottom = jnp.logical_not(jnp.logical_and(s == 1, t == 1))
    for f in range(4):
        for r in range(4):
            tile = panel[f, r].astype(F32)
            if r == 0:
                tile = jnp.where(top, tile, 0.0)
            if r == 3:
                tile = jnp.where(bottom, tile, 0.0)
            left = jnp.where(lane == 0, 0.0, pltpu.roll(tile, 1, 1))
            right = jnp.where(lane == WIDE - 1, 0.0, pltpu.roll(tile, WIDE - 1, 1))
            for b, value in enumerate((left, tile, right)):
                value = value.astype(BF16)
                for a in range(3):
                    row = r - a
                    if row in (0, 1):
                        start = 16 * (3 * a + b)
                        patches[f, start : start + 16, row * WIDE : (row + 1) * WIDE] = value

    def inverse_rms(square):
        return lax.rsqrt(jnp.sum(square, axis=0, keepdims=True) / ch + EPS)

    tiles = [slice(c, c + 16) for c in range(0, ch, 16)]

    for f in range(4):
        wide = dot(in_t[...], patches[f])
        head_sum[f] = wide[ch : ch + 16]
        square = jnp.zeros((16, PAIR), F32)
        for c in tiles:
            x = wide[c]
            first[f, c, :] = x
            square = square + x * x
        scale = inverse_rms(square)
        for c in tiles:
            normal[f, c, :] = (first[f, c, :] * scale).astype(BF16)

    def make_query(f):
        query[f] = dot(qk_t[...], normal[f]).astype(BF16)

    def attend(f):
        accs = [jnp.zeros((16, PAIR), F32)] * (f + 1)
        for c in range(0, ch, 64):
            for g in range(f + 1):
                p = [
                    query[f, i : i + 16, :] * normal[g, i : i + 16, :]
                    for i in range(c, c + 64, 16)
                ]
                accs[g] = accs[g] + ((p[0] + p[1]) + (p[2] + p[3])).astype(F32)
        scores = [jnp.sum(acc, axis=0, keepdims=True) * (1.0 / math.sqrt(ch)) for acc in accs]
        highest = functools.reduce(jnp.maximum, scores)
        weights = [jnp.exp(x - highest) for x in scores]
        norm = 1.0 / functools.reduce(jnp.add, weights)
        weights = [jnp.broadcast_to(w * norm, (16, PAIR)).astype(BF16) for w in weights]
        for c in tiles:
            mixed[f, c, :] = functools.reduce(
                jnp.add, [w * normal[g, c, :] for g, w in enumerate(weights)]
            )

    def activate(f):
        wide = dot(vo_t[...], mixed[f])
        head = head_sum[f] + wide[ch : ch + 16]
        for row in range(2):
            spot = (1, f, row + 1)
            parts[spot] = parts[spot] + head[:, row * WIDE : (row + 1) * WIDE]
        square = jnp.zeros((16, PAIR), F32)
        for c in tiles:
            x = first[f, c, :] + wide[c]
            first[f, c, :] = x
            square = square + x * x
        scale = inverse_rms(square) * 0.5
        for c in tiles:
            x = first[f, c, :] * scale
            active[f, c, :] = (x + x * jnp.tanh(x)).astype(BF16)

    def spread(f):
        wide = dot(eff[...].reshape(432, ch), active[f])
        for a in range(3):
            for b in range(3):
                for k in range(3):
                    start = 16 * (9 * a + 3 * b + k)
                    for row in range(2):
                        here = slice(row * WIDE, (row + 1) * WIDE)
                        spot = (b, f + 2 - k, row + 2 - a)
                        parts[spot] = parts[spot] + wide[start : start + 16, here]

    make_query(0)
    for f in range(4):
        if f < 3:
            make_query(f + 1)
        attend(f)
        activate(f)
        if f > 0:
            spread(f - 1)
    spread(3)

    for f in range(4):
        for r in range(4):
            left = jnp.where(lane == 0, 0.0, pltpu.roll(parts[0, f, r], 1, 1))
            right = jnp.where(lane == WIDE - 1, 0.0, pltpu.roll(parts[2, f, r], WIDE - 1, 1))
            value = parts[1, f, r] + left + right
            total[f, r] = value
            total16[f, r] = value.astype(BF16)

    sems = (o_send, o_recv)
    coeffs = [
        exchange(0, total16.at[pl.ds(2 * (1 - t), 2), pl.ds(1 - t, 3)], from_tm, x_peers[0], sems),
        exchange(1, total16.at[frames, 3 * t], from_edge.at[0], x_peers[1], sems),
        exchange(2, total16.at[pl.ds(2 * (1 - t), 2), 3 * t], from_edge.at[1], x_peers[2], sems),
    ]
    owned[...] = jnp.zeros(owned.shape, F32)
    for f in range(2):
        for r in range(3):
            owned[f, t + r] = total[2 * t + f, 1 - t + r]
    for copy in coeffs:
        copy.wait_recv()
    which = jnp.where(s == t, 0, 1)
    for f in range(2):
        for r in range(3):
            owned[f, 1 - t + r] = owned[f, 1 - t + r] + from_tm[f, r].astype(F32)
        edge = from_edge[which, f].astype(F32)
        owned[f, 3 * (1 - s)] = owned[f, 3 * (1 - s)] + edge

    for f in range(2):
        for h in range(4):
            low, high = owned[f, h, 0:8, :], owned[f, h, 8:16, :]
            for i, value in enumerate((low + high, low - high)):
                at = pl.ds(32 * f + 2 * h + i, 4, stride=8)
                pixel_rows[0, at, :] = (value[0:4] + value[4:8]) * 0.5
                pixel_rows[1, at, :] = (value[0:4] - value[4:8]) * 0.5
    both = jnp.concatenate([pixel_rows[0], pixel_rows[1]], axis=1)
    big = both.astype(BF16)
    small = (both - big.astype(F32)).astype(BF16)
    image = dot(big, spread_cols[...]) + dot(small, spread_cols[...])
    for f in range(2):
        keep = jnp.where(2 * t + f < live, 1.0, 0.0).astype(F32)
        for colour in range(3):
            start = 32 * f + 8 * colour
            out[0, f, colour] = image[start : start + 8] * keep

    for row in gathers:
        for copy in row:
            copy.wait_send()
    for copy in passes + rows + coeffs:
        copy.wait_send()


def solution(mesh):
    clips = mesh.shape["clip"]
    plane = 1 << (clips.bit_length() // 2)
    planes = clips // plane
    most = max(plane, planes)

    def body(
        gen_latent,
        frame_counts,
        owner_map,
        w_in,
        w_query,
        w_key,
        w_value,
        w_out,
        w_space,
        w_time,
        w_head,
    ):
        ch = w_query.shape[0]
        lat = jnp.swapaxes(gen_latent, -1, -2)[0]
        flat_in = w_in.reshape(144, ch)
        flat_space = w_space.reshape(9, ch, ch)
        vm = pltpu.VMEM
        dma = pltpu.SemaphoreType.DMA
        scratch = [
            vm((144, ch), BF16),
            vm((ch, ch), BF16),
            vm((ch, ch), BF16),
            vm((ch, ch), BF16),
            vm((ch, ch), BF16),
            vm((9, ch, ch), BF16),
            vm((3, ch, ch), BF16),
            vm((12, ch), BF16),
            vm((ch + 16, 144), BF16),
            vm((16, ch), BF16),
            vm((ch, ch), BF16),
            vm((ch + 16, ch), BF16),
            vm((48, ch), BF16),
            vm((9, 48, ch), BF16),
            vm((PAIR, PAIR), BF16),
            vm((planes, 4, 16, WIDE), BF16),
            vm((plane, 4, 16, WIDE), BF16),
            vm((2, most, 4, 16, WIDE), BF16),
            vm((plane, 4, 16, WIDE), BF16),
            vm((planes, 4, 16, WIDE), BF16),
            vm((2, 4, 16, WIDE), BF16),
            vm((4, 4, 16, WIDE), BF16),
            vm((4, 144, PAIR), BF16),
            vm((4, ch, PAIR), F32),
            vm((4, ch, PAIR), BF16),
            vm((4, ch, PAIR), BF16),
            vm((4, ch, PAIR), BF16),
            vm((4, ch, PAIR), BF16),
            vm((4, 16, PAIR), F32),
            vm((3, 6, 4, 16, WIDE), F32),
            vm((4, 4, 16, WIDE), F32),
            vm((4, 4, 16, WIDE), BF16),
            vm((2, 3, 16, WIDE), BF16),
            vm((2, 2, 16, WIDE), BF16),
            vm((2, 4, 16, WIDE), F32),
            vm((2, 64, WIDE), F32),
            dma((8,)),
            dma((2,)),
            dma((2, most)),
            dma((2, most)),
            dma((2, most)),
            dma((2, most)),
            dma((3,)),
            dma((3,)),
            dma((3,)),
            dma((3,)),
        ]
        hbm = pl.BlockSpec(memory_space=pltpu.HBM)
        smem = pl.BlockSpec(memory_space=pltpu.SMEM)
        return pl.pallas_call(
            functools.partial(kernel, plane, planes),
            out_shape=jax.ShapeDtypeStruct((1, 2, 3, 8, 2 * WIDE), F32),
            in_specs=[smem, smem] + [hbm] * 9,
            out_specs=pl.BlockSpec(memory_space=pltpu.VMEM),
            scratch_shapes=scratch,
            compiler_params=pltpu.CompilerParams(
                collective_id=0, has_side_effects=True, vmem_limit_bytes=64 * 1024 * 1024 - 65536
            ),
        )(
            owner_map,
            frame_counts,
            lat,
            flat_in,
            w_query,
            w_key,
            w_value,
            w_out,
            flat_space,
            w_time,
            w_head.T,
        )

    return jax.shard_map(
        body,
        mesh=mesh,
        in_specs=(P("clip", "tm", "space", None, None),) + (P(),) * 10,
        out_specs=P("clip", "tm", None, "space", None),
        check_vma=False,
    )
```

time: 257 us -> 32.2 us (0.13)
  waiting for transfers between devices: 183 us -> 0 us
  matrix products: 37.3 us -> 0 us
  Pallas kernels: 0 us -> 30.6 us
  between operations: 13.5 us -> 0.01 us
  starting transfers between devices: 13.3 us -> 0 us
  other arithmetic: 5.36 us -> 0 us
    all_gather x3 -> x0, waiting for transfers between devices: 147 us -> none  [the longest x1 83.1 us: body(): lax.all_gather(gen_latent, 'clip', axis=0, tiled=True)]
    dot_general x28 -> x0, matrix products: 37.3 us -> none  [the longest x18 13.2 us: spatial_conv(): jnp.dot(window, weight[row_step, col_step], preferred_element_type=jnp.fl...]
    ppermute x5 -> x0, waiting for transfers between devices: 35.2 us -> none  [the longest x1 22.3 us: shifted(): return lax.ppermute(block, axis, route)]
    pallas_call x0 -> x1, Pallas kernels: none -> 30.6 us  [body(): pl.pallas_call(functools.partial(kernel, plane, planes), out_shape=jax.Sh...]
    ppermute x5 -> x0, starting transfers between devices: 13 us -> none  [the longest x2 8.78 us: with_halo(): lax.ppermute(lax.slice_in_dim(block, block.shape[dim] - width, None, axis...]
  transfers between devices with their start and end apart: 8 -> 0, of which waited for: 7 -> 0; matrix products, arithmetic and copies ran while one was open for 6% -> 0% of each run, Pallas kernels for 0% -> 0%
where the time goes in v1:
time: 32.2 us; the launch traced here: 32.1 us
  Pallas kernels  30.6 us (95%)
  local copies, waits for them, and re-layouts  1.42 us (4%)
    pallas_call x1, Pallas kernels, body(): pl.pallas_call(functools.partial(kernel, plane, planes), out_shape=jax.Sh...  30.6 us
    unnamed x1, local copies, waits for them, and re-layouts  1.42 us

profile of v1, /device:TPU:2, one launch (start us, length us, event | category | flops | bytes accessed | tf_op | source)
XLA Modules:
  0.0 32.1 jit_solution(10767090685443118225)
XLA Ops:
  0.0 30.6 %shard_map.109 = f32[1,2,3,8,256]{4,3,2,1,0:T(8,128)} custom-call(s32[64]{0:T(128)} %owner.1, s32[64]{0:T(128)} %counts.1, bf16[2,4,16,128]{3,2,1,0:T(8,128)(2,1)} %bitcast.8, bf16[144,512]{1,0:T(8,128)(2,1)} %bitcast.7, bf16[512,512]{1,0:T(8,128)(2,1)} %w_query.1, bf16[512,512]{1,0:T(8,128)(2,1)} %w_key.1, bf16[512,512]{1,0:T(8,128)(2,1)} %w_value.1, ...), custom_call_target="tpu_custom_call" | custom-call | tf_op jit(solution)/shard_map/pallas_call | solution.py:489
  30.6 1.4 %copy.13 = f32[1,2,3,8,256]{4,3,2,1,0:T(8,128)} copy(f32[1,2,3,8,256]{4,3,2,1,0:T(8,128)} %shard_map.109) | data formatting | bytes 98304

commit v2 on v1

--- a/solution.py
+++ b/solution.py
@@ -69,8 +69,8 @@
     active,
     head_sum,
     parts,
-    total,
-    total16,
+    to_tm,
+    to_edge,
     from_tm,
     from_edge,
     owned,
@@ -131,23 +131,6 @@
     ]
     for copy in own + loads:
         copy.start()
-    pl.semaphore_wait(barrier, len(everyone))
-
-    gathers = ([], [])
-    for c in range(2):
-        count, peer, place = ways[c]
-        for d in sorted(range(1, count), key=lambda d: -min(d, count - d)):
-            copy = pltpu.make_async_remote_copy(
-                src_ref=lat.at[c],
-                dst_ref=gat[c].at[place],
-                send_sem=g_send.at[c, d],
-                recv_sem=g_recv.at[c, d],
-                device_id=peer(d),
-                device_id_type=MESH,
-            )
-            copy.start()
-            gathers[c].append(copy)
-
     picks = ([], [])
     for d in range(plane):
         slot = base + lax.rem(m + d, plane)
@@ -162,30 +145,68 @@
             pick = jnp.where(owner[base + i] == slot, jnp.int32(i), pick)
         picks[1].append(pick)
 
-    def scan(g, carry):
-        from_a, from_b, live = carry
-        here = owner[g] == me
-        step_a = lax.rem(m - lax.rem(g, plane) + plane, plane)
-        step_b = lax.rem(z - g // plane + planes, planes)
-        return (
-            jnp.where(here, step_a, from_a),
-            jnp.where(here, step_b, from_b),
-            jnp.where(here, counts[g], live),
-        )
-
-    from_a, from_b, live = lax.fori_loop(0, plane * planes, scan, (jnp.int32(0),) * 3)
-
-    l_key.wait()
-    l_query.wait()
-    qk_t[...] = dot_nt(v_key[...], v_query[...]).astype(BF16)
-    l_value.wait()
-    l_out.wait()
-    vo_t[0:ch, :] = dot(v_value[...], v_out[...]).T.astype(BF16)
+    def products():
+        l_key.wait()
+        l_query.wait()
+        qk_t[...] = dot_nt(v_key[...], v_query[...]).astype(BF16)
+        l_value.wait()
+        l_out.wait()
+        vo_t[0:ch, :] = dot(v_value[...], v_out[...]).T.astype(BF16)
+        l_head.wait()
+        wide = v_head[...].astype(F32)
+        gap = jnp.zeros((1, ch), F32)
+        head16[...] = jnp.concatenate(
+            [wide[0:3], gap, wide[3:6], gap, wide[6:9], gap, wide[9:12], gap], axis=0
+        ).astype(BF16)
+        l_time.wait()
+        for k in range(3):
+            taps[16 * k : 16 * k + 16, :] = dot_nt(head16[...], v_time[2 - k]).astype(BF16)
+
+        l_in.wait()
+        in_t[0:ch, :] = v_in[...].astype(F32).T.astype(BF16)
+        in_t[ch : ch + 16, :] = dot_nt(head16[...], v_in[...]).astype(BF16)
+        vo_t[ch : ch + 16, :] = dot(head16[...], vo_t[0:ch, :]).astype(BF16)
+        l_space.wait()
+
+        def fold(i):
+            got = dot_nt(taps[...], v_space[i]).astype(BF16)
+            for k in range(3):
+                eff[k, i] = got[16 * k : 16 * k + 16]
+
+        for i in range(9):
+            fold(i)
+
+        r_id = lax.broadcasted_iota(jnp.int32, (PAIR, PAIR), 0)
+        c_id = lax.broadcasted_iota(jnp.int32, (PAIR, PAIR), 1)
+        goal = jnp.where(r_id < WIDE, 2 * r_id, 2 * (r_id - WIDE) + 1)
+        spread_cols[...] = jnp.where(goal == c_id, 1.0, 0.0).astype(BF16)
+        parts[...] = jnp.zeros(parts.shape, F32)
+
+    early = z + lax.rem(m, 2) + m // 2 < planes // 2
+    pl.when(early)(products)
+
+    for copy in own:
+        copy.wait()
+    pl.semaphore_wait(barrier, len(everyone))
+
+    gathers = ([], [])
+    for c in range(2):
+        count, peer, place = ways[c]
+        for d in sorted(range(1, count), key=lambda d: -min(d, count - d)):
+            copy = pltpu.make_async_remote_copy(
+                src_ref=gat[c].at[place],
+                dst_ref=gat[c].at[place],
+                send_sem=g_send.at[c, d],
+                recv_sem=g_recv.at[c, d],
+                device_id=peer(d),
+                device_id_type=MESH,
+            )
+            copy.start()
+            gathers[c].append(copy)
 
     passes = []
     for c in (1, 0):
         count, peer, _ = ways[1 - c]
-        own[c].wait()
         for copy in gathers[c]:
             copy.wait_recv()
         for d in sorted(range(count), key=lambda d: -min(d, count - d)):
@@ -205,26 +226,20 @@
             copy.start()
             passes.append(copy)
 
-    l_head.wait()
-    wide = v_head[...].astype(F32)
-    gap = jnp.zeros((1, ch), F32)
-    head16[...] = jnp.concatenate(
-        [wide[0:3], gap, wide[3:6], gap, wide[6:9], gap, wide[9:12], gap], axis=0
-    ).astype(BF16)
-    l_in.wait()
-    in_t[0:ch, :] = v_in[...].astype(F32).T.astype(BF16)
-    in_t[ch : ch + 16, :] = dot_nt(head16[...], v_in[...]).astype(BF16)
-    vo_t[ch : ch + 16, :] = dot(head16[...], vo_t[0:ch, :]).astype(BF16)
-    l_time.wait()
-    for k in range(3):
-        taps[16 * k : 16 * k + 16, :] = dot_nt(head16[...], v_time[k]).astype(BF16)
-    l_space.wait()
-
-    def fold(i, carry):
-        eff[i] = dot_nt(taps[...], v_space[i]).astype(BF16)
-        return carry
-
-    lax.fori_loop(0, 6, fold, 0)
+    def scan(g, carry):
+        from_a, from_b, live = carry
+        here = owner[g] == me
+        step_a = lax.rem(m - lax.rem(g, plane) + plane, plane)
+        step_b = lax.rem(z - g // plane + planes, planes)
+        return (
+            jnp.where(here, step_a, from_a),
+            jnp.where(here, step_b, from_b),
+            jnp.where(here, counts[g], live),
+        )
+
+    from_a, from_b, live = lax.fori_loop(0, plane * planes, scan, (jnp.int32(0),) * 3, unroll=8)
+
+    pl.when(jnp.logical_not(early))(products)
 
     for copy in passes:
         copy.wait_recv()
@@ -253,13 +268,6 @@
     for f in range(2):
         for r in range(3):
             panel[2 * t + f, 1 - t + r] = quarter[f, t + r]
-
-    lax.fori_loop(6, 9, fold, 0)
-    r_id = lax.broadcasted_iota(jnp.int32, (PAIR, PAIR), 0)
-    c_id = lax.broadcasted_iota(jnp.int32, (PAIR, PAIR), 1)
-    goal = jnp.where(r_id < WIDE, 2 * r_id, 2 * (r_id - WIDE) + 1)
-    spread_cols[...] = jnp.where(goal == c_id, 1.0, 0.0).astype(BF16)
-    parts[...] = jnp.zeros(parts.shape, F32)
 
     for copy in rows:
         copy.wait_recv()
@@ -327,7 +335,7 @@
         wide = dot(vo_t[...], mixed[f])
         head = head_sum[f] + wide[ch : ch + 16]
         for row in range(2):
-            spot = (1, f, row + 1)
+            spot = (f, row + 1)
             parts[spot] = parts[spot] + head[:, row * WIDE : (row + 1) * WIDE]
         square = jnp.zeros((16, PAIR), F32)
         for c in tiles:
@@ -340,15 +348,23 @@
             active[f, c, :] = (x + x * jnp.tanh(x)).astype(BF16)
 
     def spread(f):
-        wide = dot(eff[...].reshape(432, ch), active[f])
-        for a in range(3):
-            for b in range(3):
-                for k in range(3):
-                    start = 16 * (9 * a + 3 * b + k)
+        steps = min(3, 4 - f)
+        wide = dot(eff[0:steps].reshape(144 * steps, ch), active[f])
+        for k in range(steps):
+            for r in range(4):
+                sides = []
+                for b in range(3):
+                    pieces = []
                     for row in range(2):
-                        here = slice(row * WIDE, (row + 1) * WIDE)
-                        spot = (b, f + 2 - k, row + 2 - a)
-                        parts[spot] = parts[spot] + wide[start : start + 16, here]
+                        a = row + 2 - r
+                        if 0 <= a < 3:
+                            start = 144 * k + 16 * (3 * a + b)
+                            here = slice(row * WIDE, (row + 1) * WIDE)
+                            pieces.append(wide[start : start + 16, here])
+                    sides.append(functools.reduce(jnp.add, pieces))
+                left = jnp.where(lane == 0, 0.0, pltpu.roll(sides[0], 1, 1))
+                right = jnp.where(lane == WIDE - 1, 0.0, pltpu.roll(sides[2], WIDE - 1, 1))
+                parts[f + k, r] = parts[f + k, r] + (sides[1] + (left + right))
 
     make_query(0)
     for f in range(4):
@@ -360,24 +376,21 @@
             spread(f - 1)
     spread(3)
 
+    for f in range(2):
+        for r in range(3):
+            to_tm[f, r] = parts[2 * (1 - t) + f, 1 - t + r].astype(BF16)
     for f in range(4):
-        for r in range(4):
-            left = jnp.where(lane == 0, 0.0, pltpu.roll(parts[0, f, r], 1, 1))
-            right = jnp.where(lane == WIDE - 1, 0.0, pltpu.roll(parts[2, f, r], WIDE - 1, 1))
-            value = parts[1, f, r] + left + right
-            total[f, r] = value
-            total16[f, r] = value.astype(BF16)
-
+        to_edge[f] = parts[f, 3 * t].astype(BF16)
     sems = (o_send, o_recv)
     coeffs = [
-        exchange(0, total16.at[pl.ds(2 * (1 - t), 2), pl.ds(1 - t, 3)], from_tm, x_peers[0], sems),
-        exchange(1, total16.at[frames, 3 * t], from_edge.at[0], x_peers[1], sems),
-        exchange(2, total16.at[pl.ds(2 * (1 - t), 2), 3 * t], from_edge.at[1], x_peers[2], sems),
+        exchange(0, to_tm, from_tm, x_peers[0], sems),
+        exchange(1, to_edge.at[frames], from_edge.at[0], x_peers[1], sems),
+        exchange(2, to_edge.at[pl.ds(2 * (1 - t), 2)], from_edge.at[1], x_peers[2], sems),
     ]
     owned[...] = jnp.zeros(owned.shape, F32)
     for f in range(2):
         for r in range(3):
-            owned[f, t + r] = total[2 * t + f, 1 - t + r]
+            owned[f, t + r] = parts[2 * t + f, 1 - t + r]
     for copy in coeffs:
         copy.wait_recv()
     which = jnp.where(s == t, 0, 1)
@@ -450,7 +463,7 @@
             vm((ch, ch), BF16),
             vm((ch + 16, ch), BF16),
             vm((48, ch), BF16),
-            vm((9, 48, ch), BF16),
+            vm((3, 9, 16, ch), BF16),
             vm((PAIR, PAIR), BF16),
             vm((planes, 4, 16, WIDE), BF16),
             vm((plane, 4, 16, WIDE), BF16),
@@ -466,9 +479,9 @@
             vm((4, ch, PAIR), BF16),
             vm((4, ch, PAIR), BF16),
             vm((4, 16, PAIR), F32),
-            vm((3, 6, 4, 16, WIDE), F32),
             vm((4, 4, 16, WIDE), F32),
-            vm((4, 4, 16, WIDE), BF16),
+            vm((2, 3, 16, WIDE), BF16),
+            vm((4, 16, WIDE), BF16),
             vm((2, 3, 16, WIDE), BF16),
             vm((2, 2, 16, WIDE), BF16),
             vm((2, 4, 16, WIDE), F32),
@@ -488,12 +501,12 @@
         smem = pl.BlockSpec(memory_space=pltpu.SMEM)
         return pl.pallas_call(
             functools.partial(kernel, plane, planes),
-            out_shape=jax.ShapeDtypeStruct((1, 2, 3, 8, 2 * WIDE), F32),
+            out_shape=pltpu.VMEM((1, 2, 3, 8, 2 * WIDE), F32),
             in_specs=[smem, smem] + [hbm] * 9,
             out_specs=pl.BlockSpec(memory_space=pltpu.VMEM),
             scratch_shapes=scratch,
             compiler_params=pltpu.CompilerParams(
-                collective_id=0, has_side_effects=True, vmem_limit_bytes=64 * 1024 * 1024 - 65536
+                collective_id=0, has_side_effects=True, vmem_limit_bytes=62 * 1024 * 1024
             ),
         )(
             owner_map,

time: 32.2 us -> 30.3 us (0.941)
  Pallas kernels: 30.6 us -> 29.6 us
  local copies, waits for them, and re-layouts: 1.42 us -> 0.62 us
    pallas_call x1, Pallas kernels: 30.6 us -> 29.6 us  [body(): pl.pallas_call(functools.partial(kernel, plane, planes), out_shape=pltpu....]
    unnamed x1, local copies, waits for them, and re-layouts: 1.42 us -> 0.62 us
where the time goes in v2:
time: 30.3 us; the launch traced here: 30.2 us
  Pallas kernels  29.6 us (98%)
  local copies, waits for them, and re-layouts  0.62 us (2%)
    pallas_call x1, Pallas kernels, body(): pl.pallas_call(functools.partial(kernel, plane, planes), out_shape=pltpu....  29.6 us
    unnamed x1, local copies, waits for them, and re-layouts  0.62 us

profile of v2, /device:TPU:2, one launch (start us, length us, event | category | flops | bytes accessed | tf_op | source)
XLA Modules:
  0.0 30.2 jit_solution(15187465355549048185)
XLA Ops:
  0.0 29.6 %shard_map.109 = f32[1,2,3,8,256]{4,3,2,1,0:T(8,128)S(1)} custom-call(s32[64]{0:T(128)} %owner.1, s32[64]{0:T(128)} %counts.1, bf16[2,4,16,128]{3,2,1,0:T(8,128)(2,1)} %bitcast.8, bf16[144,512]{1,0:T(8,128)(2,1)} %bitcast.7, bf16[512,512]{1,0:T(8,128)(2,1)} %w_query.1, bf16[512,512]{1,0:T(8,128)(2,1)} %w_key.1, bf16[512,512]{1,0:T(8,128)(2,1)} %w_value.1, ...), custom_call_target="tpu_custom_call" | custom-call | tf_op jit(solution)/shard_map/pallas_call | solution.py:502
  29.6 0.6 %copy.13 = f32[1,2,3,8,256]{4,3,2,1,0:T(8,128)} copy(f32[1,2,3,8,256]{4,3,2,1,0:T(8,128)S(1)} %shard_map.109) | data formatting | bytes 98304

commit v3 on v2

--- a/solution.py
+++ b/solution.py
@@ -27,8 +27,8 @@
 def kernel(
     plane,
     planes,
-    owner,
-    counts,
+    owner_hbm,
+    counts_hbm,
     lat,
     w_in,
     w_query,
@@ -47,6 +47,8 @@
     v_space,
     v_time,
     v_head,
+    owner,
+    counts,
     in_t,
     head16,
     qk_t,
@@ -129,21 +131,16 @@
     own = [
         pltpu.make_async_copy(lat.at[c], gat[c].at[ways[c][2]], own_sem.at[c]) for c in range(2)
     ]
-    for copy in own + loads:
+    tables = [
+        pltpu.make_async_copy(owner_hbm, owner, own_sem.at[2]),
+        pltpu.make_async_copy(counts_hbm, counts, own_sem.at[3]),
+    ]
+    for copy in own + tables:
         copy.start()
-    picks = ([], [])
-    for d in range(plane):
-        slot = base + lax.rem(m + d, plane)
-        pick = jnp.int32(0)
-        for i in range(planes):
-            pick = jnp.where(owner[i * plane + m] == slot, jnp.int32(i), pick)
-        picks[0].append(pick)
-    for d in range(planes):
-        slot = lax.rem(z + d, planes) * plane + m
-        pick = jnp.int32(0)
-        for i in range(plane):
-            pick = jnp.where(owner[base + i] == slot, jnp.int32(i), pick)
-        picks[1].append(pick)
+
+    def start_loads():
+        for load in loads:
+            load.start()
 
     def products():
         l_key.wait()
@@ -183,7 +180,11 @@
         parts[...] = jnp.zeros(parts.shape, F32)
 
     early = z + lax.rem(m, 2) + m // 2 < planes // 2
-    pl.when(early)(products)
+
+    @pl.when(early)
+    def _():
+        start_loads()
+        products()
 
     for copy in own:
         copy.wait()
@@ -203,6 +204,24 @@
             )
             copy.start()
             gathers[c].append(copy)
+
+    pl.when(jnp.logical_not(early))(start_loads)
+    for copy in tables:
+        copy.wait()
+
+    picks = ([], [])
+    for d in range(plane):
+        slot = base + lax.rem(m + d, plane)
+        pick = jnp.int32(0)
+        for i in range(planes):
+            pick = jnp.where(owner[i * plane + m] == slot, jnp.int32(i), pick)
+        picks[0].append(pick)
+    for d in range(planes):
+        slot = lax.rem(z + d, planes) * plane + m
+        pick = jnp.int32(0)
+        for i in range(plane):
+            pick = jnp.where(owner[base + i] == slot, jnp.int32(i), pick)
+        picks[1].append(pick)
 
     passes = []
     for c in (1, 0):
@@ -458,6 +477,8 @@
             vm((9, ch, ch), BF16),
             vm((3, ch, ch), BF16),
             vm((12, ch), BF16),
+            pltpu.SMEM((clips,), jnp.int32),
+            pltpu.SMEM((clips,), jnp.int32),
             vm((ch + 16, 144), BF16),
             vm((16, ch), BF16),
             vm((ch, ch), BF16),
@@ -487,7 +508,7 @@
             vm((2, 4, 16, WIDE), F32),
             vm((2, 64, WIDE), F32),
             dma((8,)),
-            dma((2,)),
+            dma((4,)),
             dma((2, most)),
             dma((2, most)),
             dma((2, most)),
@@ -498,11 +519,10 @@
             dma((3,)),
         ]
         hbm = pl.BlockSpec(memory_space=pltpu.HBM)
-        smem = pl.BlockSpec(memory_space=pltpu.SMEM)
         return pl.pallas_call(
             functools.partial(kernel, plane, planes),
             out_shape=pltpu.VMEM((1, 2, 3, 8, 2 * WIDE), F32),
-            in_specs=[smem, smem] + [hbm] * 9,
+            in_specs=[hbm] * 11,
             out_specs=pl.BlockSpec(memory_space=pltpu.VMEM),
             scratch_shapes=scratch,
             compiler_params=pltpu.CompilerParams(

time: 30.3 us -> 29.6 us (0.977)
  Pallas kernels: 29.6 us -> 28.8 us
    pallas_call x1, Pallas kernels: 29.6 us -> 28.8 us  [body(): pl.pallas_call(functools.partial(kernel, plane, planes), out_shape=pltpu....]
where the time goes in v3:
time: 29.6 us; the launch traced here: 29.4 us
  Pallas kernels  28.8 us (97%)
  local copies, waits for them, and re-layouts  0.62 us (2%)
    pallas_call x1, Pallas kernels, body(): pl.pallas_call(functools.partial(kernel, plane, planes), out_shape=pltpu....  28.8 us
    unnamed x1, local copies, waits for them, and re-layouts  0.62 us

profile of v3, /device:TPU:2, one launch (start us, length us, event | category | flops | bytes accessed | tf_op | source)
XLA Modules:
  0.0 29.4 jit_solution(8947760486715404409)
XLA Ops:
  0.0 28.8 %shard_map.109 = f32[1,2,3,8,256]{4,3,2,1,0:T(8,128)S(1)} custom-call(s32[64]{0:T(128)} %owner_hbm.1, s32[64]{0:T(128)} %counts_hbm.1, bf16[2,4,16,128]{3,2,1,0:T(8,128)(2,1)} %bitcast.8, bf16[144,512]{1,0:T(8,128)(2,1)} %bitcast.7, bf16[512,512]{1,0:T(8,128)(2,1)} %w_query.1, bf16[512,512]{1,0:T(8,128)(2,1)} %w_key.1, bf16[512,512]{1,0:T(8,128)(2,1)} %w_value.1, ...), custom_call_target="tpu_custom_call" | custom-call | tf_op jit(solution)/shard_map/pallas_call | solution.py:522
  28.8 0.6 %copy.13 = f32[1,2,3,8,256]{4,3,2,1,0:T(8,128)} copy(f32[1,2,3,8,256]{4,3,2,1,0:T(8,128)S(1)} %shard_map.109) | data formatting | bytes 98304

commit v4 on v3

--- a/solution.py
+++ b/solution.py
@@ -65,11 +65,11 @@
     panel,
     patches,
     first,
+    second,
     normal,
     query,
     mixed,
     active,
-    head_sum,
     parts,
     to_tm,
     to_edge,
@@ -317,18 +317,16 @@
     tiles = [slice(c, c + 16) for c in range(0, ch, 16)]
 
     for f in range(4):
-        wide = dot(in_t[...], patches[f])
-        head_sum[f] = wide[ch : ch + 16]
+        first[f] = dot(in_t[...], patches[f])
+
+    def make_query(f):
         square = jnp.zeros((16, PAIR), F32)
         for c in tiles:
-            x = wide[c]
-            first[f, c, :] = x
+            x = first[f, c, :]
             square = square + x * x
         scale = inverse_rms(square)
         for c in tiles:
             normal[f, c, :] = (first[f, c, :] * scale).astype(BF16)
-
-    def make_query(f):
         query[f] = dot(qk_t[...], normal[f]).astype(BF16)
 
     def attend(f):
@@ -350,21 +348,23 @@
                 jnp.add, [w * normal[g, c, :] for g, w in enumerate(weights)]
             )
 
+    def project(f):
+        second[f] = dot(vo_t[...], mixed[f])
+
     def activate(f):
-        wide = dot(vo_t[...], mixed[f])
-        head = head_sum[f] + wide[ch : ch + 16]
-        for row in range(2):
-            spot = (f, row + 1)
-            parts[spot] = parts[spot] + head[:, row * WIDE : (row + 1) * WIDE]
         square = jnp.zeros((16, PAIR), F32)
         for c in tiles:
-            x = first[f, c, :] + wide[c]
-            first[f, c, :] = x
+            x = first[f, c, :] + second[f, c, :]
+            second[f, c, :] = x
             square = square + x * x
         scale = inverse_rms(square) * 0.5
         for c in tiles:
-            x = first[f, c, :] * scale
+            x = second[f, c, :] * scale
             active[f, c, :] = (x + x * jnp.tanh(x)).astype(BF16)
+        for row in range(2):
+            here = slice(row * WIDE, (row + 1) * WIDE)
+            head = first[f, ch : ch + 16, here] + second[f, ch : ch + 16, here]
+            parts[f, row + 1] = parts[f, row + 1] + head
 
     def spread(f):
         steps = min(3, 4 - f)
@@ -385,14 +385,23 @@
                 right = jnp.where(lane == WIDE - 1, 0.0, pltpu.roll(sides[2], WIDE - 1, 1))
                 parts[f + k, r] = parts[f + k, r] + (sides[1] + (left + right))
 
-    make_query(0)
     for f in range(4):
-        if f < 3:
-            make_query(f + 1)
-        attend(f)
-        activate(f)
-        if f > 0:
-            spread(f - 1)
+        make_query(f)
+    attend(0)
+    project(0)
+    attend(1)
+    project(1)
+    activate(0)
+    attend(2)
+    project(2)
+    spread(0)
+    activate(1)
+    attend(3)
+    project(3)
+    spread(1)
+    activate(2)
+    spread(2)
+    activate(3)
     spread(3)
 
     for f in range(2):
@@ -494,12 +503,12 @@
             vm((2, 4, 16, WIDE), BF16),
             vm((4, 4, 16, WIDE), BF16),
             vm((4, 144, PAIR), BF16),
-            vm((4, ch, PAIR), F32),
+            vm((4, ch + 16, PAIR), F32),
+            vm((4, ch + 16, PAIR), F32),
             vm((4, ch, PAIR), BF16),
             vm((4, ch, PAIR), BF16),
             vm((4, ch, PAIR), BF16),
             vm((4, ch, PAIR), BF16),
-            vm((4, 16, PAIR), F32),
             vm((4, 4, 16, WIDE), F32),
             vm((2, 3, 16, WIDE), BF16),
             vm((4, 16, WIDE), BF16),

time: 29.6 us -> 29.4 us (level)
  no operation moved by 1% of the time
where the time goes in v4:
time: 29.4 us; the launch traced here: 29.2 us
  Pallas kernels  28.6 us (97%)
  local copies, waits for them, and re-layouts  0.62 us (2%)
    pallas_call x1, Pallas kernels, body(): pl.pallas_call(functools.partial(kernel, plane, planes), out_shape=pltpu....  28.6 us
    unnamed x1, local copies, waits for them, and re-layouts  0.62 us

profile of v4, /device:TPU:2, one launch (start us, length us, event | category | flops | bytes accessed | tf_op | source)
XLA Modules:
  0.0 29.2 jit_solution(6021081933718862536)
XLA Ops:
  0.0 28.6 %shard_map.109 = f32[1,2,3,8,256]{4,3,2,1,0:T(8,128)S(1)} custom-call(s32[64]{0:T(128)} %owner_hbm.1, s32[64]{0:T(128)} %counts_hbm.1, bf16[2,4,16,128]{3,2,1,0:T(8,128)(2,1)} %bitcast.8, bf16[144,512]{1,0:T(8,128)(2,1)} %bitcast.7, bf16[512,512]{1,0:T(8,128)(2,1)} %w_query.1, bf16[512,512]{1,0:T(8,128)(2,1)} %w_key.1, bf16[512,512]{1,0:T(8,128)(2,1)} %w_value.1, ...), custom_call_target="tpu_custom_call" | custom-call | tf_op jit(solution)/shard_map/pallas_call | solution.py:531
  28.6 0.6 %copy.13 = f32[1,2,3,8,256]{4,3,2,1,0:T(8,128)} copy(f32[1,2,3,8,256]{4,3,2,1,0:T(8,128)S(1)} %shard_map.109) | data formatting | bytes 98304

commit v5 on v4

--- a/solution.py
+++ b/solution.py
@@ -115,15 +115,18 @@
     ]
     l_key, l_query, l_value, l_out, l_head, l_in, l_time, l_space = loads
 
-    def plane_peer(d):
-        return (base + lax.rem(m + d, plane), s, t)
-
-    def column_peer(d):
-        return (lax.rem(z + d, planes) * plane + m, s, t)
+    def others(count, place):
+        return [i + (i + count - place) // count for i in range(count - 1)]
+
+    def plane_peer(q):
+        return (base + q, s, t)
+
+    def column_peer(q):
+        return (q * plane + m, s, t)
 
     x_peers = [(me, s, 1 - t), (me, 1 - s, t), (me, 1 - s, 1 - t)]
-    everyone = [plane_peer(d) for d in range(1, plane)]
-    everyone += [column_peer(d) for d in range(1, planes)] + x_peers
+    everyone = [plane_peer(q) for q in others(plane, m)]
+    everyone += [column_peer(q) for q in others(planes, z)] + x_peers
     barrier = pltpu.get_barrier_semaphore()
     for peer in everyone:
         pl.semaphore_signal(barrier, inc=1, device_id=peer, device_id_type=MESH)
@@ -181,78 +184,74 @@
 
     early = z + lax.rem(m, 2) + m // 2 < planes // 2
 
-    @pl.when(early)
-    def _():
-        start_loads()
-        products()
+    last = jnp.logical_and(z >= planes // 2, m >= plane // 2)
+    pl.when(jnp.logical_not(last))(start_loads)
+    pl.when(early)(products)
 
     for copy in own:
         copy.wait()
     pl.semaphore_wait(barrier, len(everyone))
 
-    gathers = ([], [])
+    def send(i, src, dst, sems, place, device):
+        copy = pltpu.make_async_remote_copy(
+            src_ref=src,
+            dst_ref=dst,
+            send_sem=sems[0].at[i],
+            recv_sem=sems[1].at[place],
+            device_id=device,
+            device_id_type=MESH,
+        )
+        copy.start()
+        return copy
+
+    def arrive(dst, sems, place, device):
+        pltpu.make_async_remote_copy(
+            src_ref=dst,
+            dst_ref=dst,
+            send_sem=sems[0].at[0],
+            recv_sem=sems[1].at[place],
+            device_id=device,
+            device_id_type=MESH,
+        ).wait_recv()
+
+    sent = []
     for c in range(2):
         count, peer, place = ways[c]
-        for d in sorted(range(1, count), key=lambda d: -min(d, count - d)):
-            copy = pltpu.make_async_remote_copy(
-                src_ref=gat[c].at[place],
-                dst_ref=gat[c].at[place],
-                send_sem=g_send.at[c, d],
-                recv_sem=g_recv.at[c, d],
-                device_id=peer(d),
-                device_id_type=MESH,
-            )
-            copy.start()
-            gathers[c].append(copy)
-
-    pl.when(jnp.logical_not(early))(start_loads)
+        sems = (g_send.at[c], g_recv.at[c])
+        block = gat[c].at[place]
+        for i, q in enumerate(others(count, place)):
+            sent.append(send(i, block, block, sems, place, peer(q)))
+
     for copy in tables:
         copy.wait()
 
-    picks = ([], [])
-    for d in range(plane):
-        slot = base + lax.rem(m + d, plane)
-        pick = jnp.int32(0)
-        for i in range(planes):
-            pick = jnp.where(owner[i * plane + m] == slot, jnp.int32(i), pick)
-        picks[0].append(pick)
-    for d in range(planes):
-        slot = lax.rem(z + d, planes) * plane + m
-        pick = jnp.int32(0)
-        for i in range(plane):
-            pick = jnp.where(owner[base + i] == slot, jnp.int32(i), pick)
-        picks[1].append(pick)
-
-    passes = []
+    def pick(c, q):
+        found = jnp.int32(0)
+        for i in range(ways[c][0]):
+            here, goal = (i * plane + m, base + q) if c == 0 else (base + i, q * plane + m)
+            found = jnp.where(owner[here] == goal, jnp.int32(i), found)
+        return found
+
     for c in (1, 0):
-        count, peer, _ = ways[1 - c]
-        for copy in gathers[c]:
-            copy.wait_recv()
-        for d in sorted(range(count), key=lambda d: -min(d, count - d)):
-            block = gat[c][picks[c][d]]
-            if d == 0:
-                got[c][0] = block
-                continue
-            p_buf[c, d] = block
-            copy = pltpu.make_async_remote_copy(
-                src_ref=p_buf.at[c, d],
-                dst_ref=got[c].at[d],
-                send_sem=p_send.at[c, d],
-                recv_sem=p_recv.at[c, d],
-                device_id=peer(d),
-                device_id_type=MESH,
-            )
-            copy.start()
-            passes.append(copy)
+        count, peer, place = ways[c]
+        sems = (g_send.at[c], g_recv.at[c])
+        for q in others(count, place):
+            arrive(gat[c].at[q], sems, q, peer(q))
+        count, peer, place = ways[1 - c]
+        sems = (p_send.at[c], p_recv.at[c])
+        for i, q in enumerate(others(count, place)):
+            p_buf[c, i] = gat[c][pick(c, q)]
+            sent.append(send(i, p_buf.at[c, i], got[c].at[place], sems, place, peer(q)))
+        got[c][place] = gat[c][pick(c, place)]
+
+    pl.when(last)(start_loads)
 
     def scan(g, carry):
         from_a, from_b, live = carry
         here = owner[g] == me
-        step_a = lax.rem(m - lax.rem(g, plane) + plane, plane)
-        step_b = lax.rem(z - g // plane + planes, planes)
         return (
-            jnp.where(here, step_a, from_a),
-            jnp.where(here, step_b, from_b),
+            jnp.where(here, lax.rem(g, plane), from_a),
+            jnp.where(here, g // plane, from_b),
             jnp.where(here, counts[g], live),
         )
 
@@ -260,8 +259,10 @@
 
     pl.when(jnp.logical_not(early))(products)
 
-    for copy in passes:
-        copy.wait_recv()
+    for c in range(2):
+        count, peer, place = ways[1 - c]
+        for q in others(count, place):
+            arrive(got[c].at[q], (p_send.at[c], p_recv.at[c]), q, peer(q))
     quarter[0] = got_a[from_a]
     quarter[1] = got_b[from_b]
 
@@ -445,10 +446,7 @@
             start = 32 * f + 8 * colour
             out[0, f, colour] = image[start : start + 8] * keep
 
-    for row in gathers:
-        for copy in row:
-            copy.wait_send()
-    for copy in passes + rows + coeffs:
+    for copy in sent + rows + coeffs:
         copy.wait_send()
 
 

time: 29.4 us -> 29.2 us (level)
  Pallas kernels: 28.6 us -> 28.1 us
    pallas_call x1, Pallas kernels: 28.6 us -> 28.1 us  [body(): pl.pallas_call(functools.partial(kernel, plane, planes), out_shape=pltpu....]
where the time goes in v5:
time: 29.2 us; the launch traced here: 28.7 us
  Pallas kernels  28.1 us (96%)
  local copies, waits for them, and re-layouts  0.62 us (2%)
    pallas_call x1, Pallas kernels, body(): pl.pallas_call(functools.partial(kernel, plane, planes), out_shape=pltpu....  28.1 us
    unnamed x1, local copies, waits for them, and re-layouts  0.62 us

profile of v5, /device:TPU:2, one launch (start us, length us, event | category | flops | bytes accessed | tf_op | source)
XLA Modules:
  0.0 28.7 jit_solution(14362589501419575641)
XLA Ops:
  0.0 28.1 %shard_map.109 = f32[1,2,3,8,256]{4,3,2,1,0:T(8,128)S(1)} custom-call(s32[64]{0:T(128)} %owner_hbm.1, s32[64]{0:T(128)} %counts_hbm.1, bf16[2,4,16,128]{3,2,1,0:T(8,128)(2,1)} %bitcast.8, bf16[144,512]{1,0:T(8,128)(2,1)} %bitcast.7, bf16[512,512]{1,0:T(8,128)(2,1)} %w_query.1, bf16[512,512]{1,0:T(8,128)(2,1)} %w_key.1, bf16[512,512]{1,0:T(8,128)(2,1)} %w_value.1, ...), custom_call_target="tpu_custom_call" | custom-call | tf_op jit(solution)/shard_map/pallas_call | solution.py:529
  28.1 0.6 %copy.13 = f32[1,2,3,8,256]{4,3,2,1,0:T(8,128)} copy(f32[1,2,3,8,256]{4,3,2,1,0:T(8,128)S(1)} %shard_map.109) | data formatting | bytes 98304

commit v6 on v5

--- a/solution.py
+++ b/solution.py
@@ -125,14 +125,14 @@
         return (q * plane + m, s, t)
 
     x_peers = [(me, s, 1 - t), (me, 1 - s, t), (me, 1 - s, 1 - t)]
-    everyone = [plane_peer(q) for q in others(plane, m)]
-    everyone += [column_peer(q) for q in others(planes, z)] + x_peers
+    everyone = [column_peer(q) for q in others(planes, z)] + x_peers
+    everyone += [plane_peer(q) for q in others(plane, m)]
     barrier = pltpu.get_barrier_semaphore()
     for peer in everyone:
         pl.semaphore_signal(barrier, inc=1, device_id=peer, device_id_type=MESH)
     ways = ((planes, column_peer, z), (plane, plane_peer, m))
     own = [
-        pltpu.make_async_copy(lat.at[c], gat[c].at[ways[c][2]], own_sem.at[c]) for c in range(2)
+        pltpu.make_async_copy(lat.at[1 - c], gat[c].at[ways[c][2]], own_sem.at[c]) for c in range(2)
     ]
     tables = [
         pltpu.make_async_copy(owner_hbm, owner, own_sem.at[2]),
@@ -215,7 +215,7 @@
         ).wait_recv()
 
     sent = []
-    for c in range(2):
+    for c in (1, 0):
         count, peer, place = ways[c]
         sems = (g_send.at[c], g_recv.at[c])
         block = gat[c].at[place]
@@ -259,13 +259,6 @@
 
     pl.when(jnp.logical_not(early))(products)
 
-    for c in range(2):
-        count, peer, place = ways[1 - c]
-        for q in others(count, place):
-            arrive(got[c].at[q], (p_send.at[c], p_recv.at[c]), q, peer(q))
-    quarter[0] = got_a[from_a]
-    quarter[1] = got_b[from_b]
-
     def exchange(i, src, dst, peer, sems):
         copy = pltpu.make_async_remote_copy(
             src_ref=src,
@@ -279,23 +272,27 @@
         return copy
 
     frames = pl.ds(2 * t, 2)
-    sems = (x_send, x_recv)
-    rows = [
-        exchange(0, quarter.at[:, pl.ds(1 - t, 3)], panel.at[frames, pl.ds(t, 3)], x_peers[0], sems),
-        exchange(1, quarter.at[:, 3 * (1 - s)], panel.at[frames, 3 * t], x_peers[1], sems),
-        exchange(2, quarter.at[:, 3 * (1 - s)], panel.at[frames, 3 * (1 - t)], x_peers[2], sems),
-    ]
-    for f in range(2):
+    rows = []
+    for c in (1, 0):
+        count, peer, place = ways[1 - c]
+        for q in others(count, place):
+            arrive(got[c].at[q], (p_send.at[c], p_recv.at[c]), q, peer(q))
+        quarter[c] = got[c][(from_a, from_b)[c]]
+        sems = (x_send.at[1 - c], x_recv.at[1 - c])
+        near, edge = quarter.at[c, pl.ds(1 - t, 3)], quarter.at[c, 3 * (1 - s)]
+        f = 2 * t + 1 - c
+        rows += [
+            exchange(0, near, panel.at[f, pl.ds(t, 3)], x_peers[0], sems),
+            exchange(1, edge, panel.at[f, 3 * t], x_peers[1], sems),
+            exchange(2, edge, panel.at[f, 3 * (1 - t)], x_peers[2], sems),
+        ]
         for r in range(3):
-            panel[2 * t + f, 1 - t + r] = quarter[f, t + r]
-
-    for copy in rows:
-        copy.wait_recv()
+            panel[f, 1 - t + r] = quarter[c, t + r]
 
     lane = lax.broadcasted_iota(jnp.int32, (16, WIDE), 1)
     top = jnp.logical_not(jnp.logical_and(s == 0, t == 0))
     bottom = jnp.logical_not(jnp.logical_and(s == 1, t == 1))
-    for f in range(4):
+    def make_patches(f):
         for r in range(4):
             tile = panel[f, r].astype(F32)
             if r == 0:
@@ -316,9 +313,6 @@
         return lax.rsqrt(jnp.sum(square, axis=0, keepdims=True) / ch + EPS)
 
     tiles = [slice(c, c + 16) for c in range(0, ch, 16)]
-
-    for f in range(4):
-        first[f] = dot(in_t[...], patches[f])
 
     def make_query(f):
         square = jnp.zeros((16, PAIR), F32)
@@ -386,16 +380,26 @@
                 right = jnp.where(lane == WIDE - 1, 0.0, pltpu.roll(sides[2], WIDE - 1, 1))
                 parts[f + k, r] = parts[f + k, r] + (sides[1] + (left + right))
 
-    for f in range(4):
-        make_query(f)
+    def begin(c):
+        for copy in rows[3 * c : 3 * c + 3]:
+            copy.wait_recv()
+        for f in (c, c + 2):
+            make_patches(f)
+        for f in (c, c + 2):
+            first[f] = dot(in_t[...], patches[f])
+        for f in (c, c + 2):
+            make_query(f)
+
+    begin(0)
     attend(0)
     project(0)
+    activate(0)
+    spread(0)
+    begin(1)
     attend(1)
     project(1)
-    activate(0)
     attend(2)
     project(2)
-    spread(0)
     activate(1)
     attend(3)
     project(3)
@@ -420,6 +424,8 @@
     for f in range(2):
         for r in range(3):
             owned[f, t + r] = parts[2 * t + f, 1 - t + r]
+    for copy in sent + rows:
+        copy.wait_send()
     for copy in coeffs:
         copy.wait_recv()
     which = jnp.where(s == t, 0, 1)
@@ -446,7 +452,7 @@
             start = 32 * f + 8 * colour
             out[0, f, colour] = image[start : start + 8] * keep
 
-    for copy in sent + rows + coeffs:
+    for copy in coeffs:
         copy.wait_send()
 
 
@@ -520,8 +526,8 @@
             dma((2, most)),
             dma((2, most)),
             dma((2, most)),
-            dma((3,)),
-            dma((3,)),
+            dma((2, 3)),
+            dma((2, 3)),
             dma((3,)),
             dma((3,)),
         ]

time: 29.2 us -> 30.3 us (1.038)
  Pallas kernels: 28.1 us -> 29.2 us
    pallas_call x1, Pallas kernels: 28.1 us -> 29.2 us  [body(): pl.pallas_call(functools.partial(kernel, plane, planes), out_shape=pltpu....]
where the time goes in v6:
time: 30.3 us; the launch traced here: 29.8 us
  Pallas kernels  29.2 us (96%)
  local copies, waits for them, and re-layouts  0.62 us (2%)
    pallas_call x1, Pallas kernels, body(): pl.pallas_call(functools.partial(kernel, plane, planes), out_shape=pltpu....  29.2 us
    unnamed x1, local copies, waits for them, and re-layouts  0.62 us

profile of v6, /device:TPU:2, one launch (start us, length us, event | category | flops | bytes accessed | tf_op | source)
XLA Modules:
  0.0 29.8 jit_solution(10052460527645101833)
XLA Ops:
  0.0 29.2 %shard_map.109 = f32[1,2,3,8,256]{4,3,2,1,0:T(8,128)S(1)} custom-call(s32[64]{0:T(128)} %owner_hbm.1, s32[64]{0:T(128)} %counts_hbm.1, bf16[2,4,16,128]{3,2,1,0:T(8,128)(2,1)} %bitcast.8, bf16[144,512]{1,0:T(8,128)(2,1)} %bitcast.7, bf16[512,512]{1,0:T(8,128)(2,1)} %w_query.1, bf16[512,512]{1,0:T(8,128)(2,1)} %w_key.1, bf16[512,512]{1,0:T(8,128)(2,1)} %w_value.1, ...), custom_call_target="tpu_custom_call" | custom-call | tf_op jit(solution)/shard_map/pallas_call | solution.py:535
  29.2 0.6 %copy.13 = f32[1,2,3,8,256]{4,3,2,1,0:T(8,128)} copy(f32[1,2,3,8,256]{4,3,2,1,0:T(8,128)S(1)} %shard_map.109) | data formatting | bytes 98304

commit v7 on v5

--- a/solution.py
+++ b/solution.py
@@ -125,8 +125,8 @@
         return (q * plane + m, s, t)
 
     x_peers = [(me, s, 1 - t), (me, 1 - s, t), (me, 1 - s, 1 - t)]
-    everyone = [plane_peer(q) for q in others(plane, m)]
-    everyone += [column_peer(q) for q in others(planes, z)] + x_peers
+    everyone = [column_peer(q) for q in others(planes, z)] + x_peers
+    everyone += [plane_peer(q) for q in others(plane, m)]
     barrier = pltpu.get_barrier_semaphore()
     for peer in everyone:
         pl.semaphore_signal(barrier, inc=1, device_id=peer, device_id_type=MESH)
@@ -420,6 +420,8 @@
     for f in range(2):
         for r in range(3):
             owned[f, t + r] = parts[2 * t + f, 1 - t + r]
+    for copy in sent + rows:
+        copy.wait_send()
     for copy in coeffs:
         copy.wait_recv()
     which = jnp.where(s == t, 0, 1)
@@ -446,7 +448,7 @@
             start = 32 * f + 8 * colour
             out[0, f, colour] = image[start : start + 8] * keep
 
-    for copy in sent + rows + coeffs:
+    for copy in coeffs:
         copy.wait_send()
 
 

time: 29.2 us -> 29.1 us (level)
  no operation moved by 1% of the time
where the time goes in v7:
time: 29.1 us; the launch traced here: 28.6 us
  Pallas kernels  28 us (96%)
  local copies, waits for them, and re-layouts  0.62 us (2%)
    pallas_call x1, Pallas kernels, body(): pl.pallas_call(functools.partial(kernel, plane, planes), out_shape=pltpu....  28 us
    unnamed x1, local copies, waits for them, and re-layouts  0.62 us

profile of v7, /device:TPU:2, one launch (start us, length us, event | category | flops | bytes accessed | tf_op | source)
XLA Modules:
  0.0 28.6 jit_solution(10473733040927192246)
XLA Ops:
  0.0 28.0 %shard_map.109 = f32[1,2,3,8,256]{4,3,2,1,0:T(8,128)S(1)} custom-call(s32[64]{0:T(128)} %owner_hbm.1, s32[64]{0:T(128)} %counts_hbm.1, bf16[2,4,16,128]{3,2,1,0:T(8,128)(2,1)} %bitcast.8, bf16[144,512]{1,0:T(8,128)(2,1)} %bitcast.7, bf16[512,512]{1,0:T(8,128)(2,1)} %w_query.1, bf16[512,512]{1,0:T(8,128)(2,1)} %w_key.1, bf16[512,512]{1,0:T(8,128)(2,1)} %w_value.1, ...), custom_call_target="tpu_custom_call" | custom-call | tf_op jit(solution)/shard_map/pallas_call | solution.py:531
  28.0 0.6 %copy.13 = f32[1,2,3,8,256]{4,3,2,1,0:T(8,128)} copy(f32[1,2,3,8,256]{4,3,2,1,0:T(8,128)S(1)} %shard_map.109) | data formatting | bytes 98304
